TPU v7x, 128 devices: a whole 4x4x4 slice. The times are simulated.
128 devices in a mesh: seq: 16 (over x, y), section: 8 (over z, core).
Axes of the slice: x: 4, y: 4, z: 4, core: 2. Of those that a mesh axis runs over, the one named last changes fastest.
Arguments:
- hidden: bfloat16 [8, 6144, 2560], P('section', 'seq'), may hold values from -6 to 6
- query_norm_gain: float32 [8, 2560], P('section'), may hold values from 0.25 to 1.75
- key_norm_gain: float32 [8, 2560], P('section'), may hold values from 0.25 to 1.75
- text_kv: bfloat16 [8, 16, 2, 512, 2560], P('section', 'seq'), may hold values from -6 to 6
- holder: int32 [8], P('section'), may hold values from 0 to 15
- pattern: int32 [48, 7], replicated, may hold values from 0 to 1, as said below
- grad_out: bfloat16 [8, 6144, 2560], P('section', 'seq'), may hold values from -6 to 6
Outputs:
- attended: bfloat16 [8, 6144, 2560], P('section', 'seq')
- upstream: bfloat16 [8, 6144, 2560], P('section', 'seq')
- text_grad: bfloat16 [8, 2, 512, 2560], P('section')
Inputs may be any that keep to these rules, and one draw needn't show every extreme that they name: pattern[b, 3] = 1 for every block b; entries are 0 or 1.
All inputs are finite; a program needn't handle non-finite values.
Results may differ from a plain program's by a relative error of at most 0.0078.
Values may be sent and summed in bfloat16 or wider, within the bound.
A program may use at most 256 MiB of HBM per device.

v0:
```python
import jax
import jax.numpy as jnp
from jax import lax
from jax.sharding import PartitionSpec as P

HDIM = 128
BLK = 128
eps = 1e-06


def extended(cells, sides, width):
    for axis, dim in sides:
        count = lax.axis_size(axis)
        ends = count - 1
        head = lax.slice_in_dim(cells, 0, width, axis=dim)
        tail = lax.slice_in_dim(cells, cells.shape[dim] - width, cells.shape[dim], axis=dim)
        cells = jnp.concatenate(
            [
                lax.ppermute(tail, axis, [(i, (i + 1) % count) for i in range(ends)]),
                cells,
                lax.ppermute(head, axis, [((i + 1) % count, i) for i in range(ends)]),
            ],
            axis=dim,
        )
    return cells


def from_root(block, axis, owner):
    block = jnp.where(lax.axis_index(axis) == owner, block, jnp.zeros_like(block))
    return lax.psum(block, axis)


def shifted(x, axis, by):
    peers = lax.axis_size(axis)
    pairs = [(i, i + by) for i in range(peers) if 0 <= i + by < peers]
    return lax.ppermute(x, axis, pairs)


def norm_forward(hidden_state, norm_gain):
    hidden_float = hidden_state.astype(jnp.float32)
    inverse_root_norm = lax.rsqrt(
        jnp.mean(hidden_float * hidden_float, axis=-1, keepdims=True) + eps
    )
    normalized_input = hidden_float * inverse_root_norm
    return (
        (normalized_input * norm_gain).astype(jnp.bfloat16),
        normalized_input,
        inverse_root_norm,
    )


def norm_backward(upper_bound, norm_gain, normalized_input, inverse_root_norm):
    scaled_input = upper_bound * norm_gain
    return inverse_root_norm * (
        scaled_input
        - normalized_input * jnp.mean(scaled_input * normalized_input, axis=-1, keepdims=True)
    )


def block_mask(pattern, slab, bpd, nslab):
    span = pattern.shape[1]
    rows = lax.dynamic_slice_in_dim(pattern, slab * bpd, bpd, 0)
    first = jnp.arange(bpd, dtype=jnp.int32)[:, None]
    second = jnp.arange(3 * bpd, dtype=jnp.int32)[None, :]
    offset = second - first
    onehot = offset[:, :, None] == jnp.arange(span, dtype=jnp.int32)[None, None, :]
    picked = jnp.sum(jnp.where(onehot, rows[:, None, :], 0), axis=-1)
    globe = slab * bpd - bpd + second
    inside = (globe >= 0) & (globe < nslab * bpd)
    return (picked > 0) & inside


def token_mask(blocks):
    return jnp.repeat(jnp.repeat(blocks, BLK, axis=0), BLK, axis=1)


def divide_heads(x):
    return x.reshape(x.shape[0], x.shape[1] // HDIM, HDIM).transpose(1, 0, 2)


def join_heads(x):
    return x.transpose(1, 0, 2).reshape(x.shape[1], x.shape[0] * x.shape[2])


def query_side(qh, kh, vh, tkh, tvh, doh, attend_mask):
    scale = qh.shape[-1] ** (-0.5)
    keys = jnp.concatenate([kh, tkh], axis=0)
    vals = jnp.concatenate([vh, tvh], axis=0)
    full = jnp.concatenate([attend_mask, jnp.ones((qh.shape[0], tkh.shape[0]), bool)], axis=1)
    scores = jnp.dot(qh, keys.T, preferred_element_type=jnp.float32) * scale
    scores = jnp.where(full, scores, -1e30)
    top = jnp.max(scores, axis=1, keepdims=True)
    total = jnp.sum(jnp.where(full, jnp.exp(scores - top), 0.0), axis=1, keepdims=True)
    lse = top + jnp.log(total)
    probs = jnp.where(full, jnp.exp(scores - lse), 0.0)
    probs_b = probs.astype(jnp.bfloat16)
    out = jnp.dot(probs_b, vals, preferred_element_type=jnp.float32)
    dprob = jnp.dot(doh, vals.T, preferred_element_type=jnp.float32)
    delta = jnp.sum(doh.astype(jnp.float32) * out, axis=1)
    dscore = (probs * (dprob - delta[:, None]) * scale).astype(jnp.bfloat16)
    query_gradient = jnp.dot(dscore, keys, preferred_element_type=jnp.float32)
    dkeys = jnp.dot(dscore.T, qh, preferred_element_type=jnp.float32)
    dvals = jnp.dot(probs_b.T, doh, preferred_element_type=jnp.float32)
    return (out, lse[:, 0], delta, query_gradient, dkeys, dvals)


def local(hidden, query_norm_gain, key_norm_gain, text_kv, holder, pattern, grad_out):
    hidden_state = hidden[0]
    output_gradient = grad_out[0]
    token_rows = hidden_state.shape[0]
    bpd = token_rows // BLK
    slab = lax.axis_index("seq")
    nslab = lax.axis_size("seq")
    normed_query, normalized_input, inverse_root_norm = norm_forward(
        hidden_state, query_norm_gain[0]
    )
    kn, _, _ = norm_forward(hidden_state, key_norm_gain[0])
    near = extended(jnp.stack([kn, hidden_state]), (("seq", 1),), token_rows)
    text_tokens = from_root(text_kv[0, 0], "seq", holder[0])
    attend_mask = token_mask(block_mask(pattern, slab, bpd, nslab))

    def each_head_value(a):
        return query_side(a[0], a[1], a[2], a[3], a[4], a[5], attend_mask)

    saved_residuals = lax.map(
        each_head_value,
        (
            divide_heads(normed_query),
            divide_heads(near[0]),
            divide_heads(near[1]),
            divide_heads(text_tokens[0]),
            divide_heads(text_tokens[1]),
            divide_heads(output_gradient),
        ),
    )
    out, lse, delta, query_gradient, dkeys, dvals = saved_residuals
    ext_rows = 3 * token_rows
    dtext_part = jnp.stack([join_heads(dkeys[:, ext_rows:]), join_heads(dvals[:, ext_rows:])])
    ext = jnp.stack([join_heads(dkeys[:, :ext_rows]), join_heads(dvals[:, :ext_rows])])
    from_upper = shifted(ext[:, :token_rows].astype(jnp.bfloat16), "seq", -1).astype(jnp.float32)
    from_lower = shifted(ext[:, 2 * token_rows :].astype(jnp.bfloat16), "seq", 1).astype(
        jnp.float32
    )
    own_rows = ext[:, token_rows : 2 * token_rows] + from_upper + from_lower
    text_total = lax.psum(dtext_part, "seq")
    grad_hidden = (
        own_rows[1]
        + norm_backward(
            join_heads(query_gradient), query_norm_gain[0], normalized_input, inverse_root_norm
        )
        + norm_backward(own_rows[0], key_norm_gain[0], normalized_input, inverse_root_norm)
    )
    upstream = shifted(grad_hidden.astype(jnp.bfloat16), "section", -1)
    attended = join_heads(out).astype(jnp.bfloat16)
    return (attended[None], upstream[None], text_total.astype(jnp.bfloat16)[None])


def solution(mesh):
    in_specs = (
        P("section", "seq", None),
        P("section", None),
        P("section", None),
        P("section", "seq", None, None, None),
        P("section"),
        P(),
        P("section", "seq", None),
    )
    out_specs = (
        P("section", "seq", None),
        P("section", "seq", None),
        P("section", None, None, None),
    )
    return jax.shard_map(local, mesh=mesh, in_specs=in_specs, out_specs=out_specs, check_vma=False)
```

profile of v0, /device:TPU:24, one launch (start us, length us, event | category | flops | bytes accessed | tf_op | source)
XLA Modules:
  0.0 923.3 jit_solution(16334344849139469414)
XLA Ops:
  17.4 5.3 collective-permute-start
  23.4 8.0 copy.45
  34.7 4.0 copy.46
  38.7 3.2 fusion.42
  41.9 93.5 %collective-permute-done.1 = bf16[2,384,2560]{1,2,0:T(8,128)(2,1)} collective-permute-done((bf16[2,384,2560]{1,2,0:T(8,128)(2,1)}, bf16[2,384,2560]{1,2,0:T(8,128)(2,1)}, u32[]{:S(2)}, u32[]{:S(2)}) %collective-permute-start.1) | collective-permute-done | bytes 3932192 | tf_op jit(solution)/shard_map/ppermute | solution.py:21
  138.5 5.1 pad_maximum_fusion.7
  143.7 4.9 fusion.45
  148.6 26.1 %all-reduce.4.cloned.1.call-done = bf16[2,512,2560]{1,2,0:T(8,128)(2,1)} async-done(((bf16[2,512,2560]{1,2,0:T(8,128)(2,1)}), bf16[2,512,2560]{1,2,0:T(8,128)(2,1)}) %all-reduce.4.cloned.1.call-update) | async-done | bytes 5242896 | tf_op jit(solution)/shard_map/psum | solution.py:30
  174.6 5.2 fusion.46
  179.8 351.3 %while.17 = (s32[]{:T(128)}, bf16[20,384,128]{1,2,0:T(8,128)(2,1)}, f32[20,384,128]{1,2,0:T(8,128)}, f32[20,1664,128]{1,2,0:T(8,128)}, f32[20,1664,128]{1,2,0:T(...) while((s32[]{:T(128)}, bf16[20,384,128]{1,2,0:T(8,128)(2,1)}, ...), condition=%wide.region_7.8_spmd.clone, body=%wide.region_3.7_spmd.clone.sunk | while | flops 996523264 | bytes 28792892 | solution.py:125
  531.1 9.7 %slice.46 = f32[20,1152,128]{1,2,0:T(8,128)} slice(f32[20,1664,128]{1,2,0:T(8,128)} %get-tuple-element.70), slice={[0:20], [0:1152], [0:128]} | slice | bytes 23592960 | tf_op jit(solution)/shard_map/slice | solution.py:139
  540.9 9.7 %slice.45 = f32[20,1152,128]{1,2,0:T(8,128)} slice(f32[20,1664,128]{1,2,0:T(8,128)} %get-tuple-element.69), slice={[0:20], [0:1152], [0:128]} | slice | bytes 23592960 | tf_op jit(solution)/shard_map/slice | solution.py:139
  550.6 9.0 fusion.29
  559.6 3.6 fusion.44
  565.9 5.4 collective-permute-start.3
  571.3 5.7 slice.53
  577.0 5.6 slice.52
  582.6 10.1 %pad_maximum_fusion.8 = f32[2,512,2560]{1,2,0:T(8,128)} fusion(f32[1,512,2560]{1,2,0:T(8,128)} %bitcast.170, f32[1,512,2560]{1,2,0:T(8,128)} %bitcast.171), kind=kLoop, calls=%fused_computation.47 | loop fusion | flops 2621440 | bytes 20971520 | tf_op jit(solution)/shard_map/stack | solution.py:138
  592.7 3.9 fusion.40
  596.7 57.5 %collective-permute-done.2 = bf16[2,384,2560]{1,2,0:T(8,128)(2,1)} collective-permute-done((bf16[2,384,2560]{1,2,0:T(8,128)(2,1)}, bf16[2,384,2560]{1,2,0:T(8,128)(2,1)}, u32[]{:S(2)}, u32[]{:S(2)}) %collective-permute-start.2) | collective-permute-done | bytes 3932192 | tf_op jit(solution)/shard_map/ppermute | solution.py:36
  655.4 5.0 fusion.32
  666.9 235.2 %all-reduce.5 = bf16[2,512,2560]{1,2,0:T(8,128)(2,1)} all-reduce(f32[2,512,2560]{1,2,0:T(8,128)} %pad_maximum_fusion.8), channel_id=1, replica_groups=mesh['seq'=16,'section'=8] {'seq'}, use_global_device_ids=true, to_apply=%region_10.11 | all-reduce | flops 2621440 | bytes 15728640 | tf_op jit(solution)/shard_map/psum | solution.py:145
  904.6 7.9 copy.62
  912.5 4.0 copy.61
  (438 shorter events, 379.8 us)
Async XLA Ops:
  7.2 26.9 %copy-start = (s32[48,7]{0,1:T(8,128)S(1)}, s32[48,7]{0,1:T(8,128)}, u32[]{:S(2)}) copy-start(s32[48,7]{0,1:T(8,128)} %param.14) | copy-start | bytes 4036
  7.2 167.4 %all-reduce.4.cloned.1.call-start = ((), (), s32[]{:S(2)}) async-start(), calls=%async_computation | async-start | bytes 10485760 | tf_op jit(solution)/shard_map/psum | solution.py:30
  14.7 120.7 %collective-permute-start.1 = (bf16[2,384,2560]{1,2,0:T(8,128)(2,1)}, bf16[2,384,2560]{1,2,0:T(8,128)(2,1)}, u32[]{:S(2)}, u32[]{:S(2)}) collective-permute-start(bf16[2,384,2560]{1,2,0:T(8,128)(2,1)} %pad_maximum_fusion.9), channel_id=1, source_target_pairs={{8,0},{16,8},{24,16},{32,24},{40,32},{48,40},{56,48},{64,56},{72,6... | collective-permute-start | bytes 11796488 | tf_op jit(solution)/shard_map/ppermute | solution.py:21
  17.4 121.1 %collective-permute-start = (bf16[2,384,2560]{1,2,0:T(8,128)(2,1)}, bf16[2,384,2560]{1,2,0:T(8,128)(2,1)}, u32[]{:S(2)}, u32[]{:S(2)}) collective-permute-start(bf16[2,384,2560]{1,2,0:T(8,128)(2,1)} %pad_maximum_fusion.9), channel_id=1, source_target_pairs={{0,8},{8,16},{16,24},{24,32},{32,40},{40,48},{48,56},{56,64},{64,7... | collective-permute-start | bytes 11796488 | tf_op jit(solution)/shard_map/ppermute | solution.py:19
  38.7 99.8 %copy-start.3 = (bf16[1,384,2560]{1,2,0:T(8,128)(2,1)S(1)}, bf16[1,384,2560]{1,2,0:T(8,128)(2,1)}, u32[]{:S(2)}) copy-start(bf16[1,384,2560]{1,2,0:T(8,128)(2,1)} %copy-done.2) | copy-start | bytes 5898244
  203.1 3.9 copy-start.5
  238.2 3.9 copy-start.5
  273.3 3.9 copy-start.5
  290.8 3.9 copy-start.5
  308.3 3.9 copy-start.5
  325.9 3.9 copy-start.5
  343.4 3.9 copy-start.5
  378.8 3.9 copy-start.5
  396.3 3.9 copy-start.5
  431.4 3.9 copy-start.5
  448.9 3.9 copy-start.5
  563.2 91.0 %collective-permute-start.2 = (bf16[2,384,2560]{1,2,0:T(8,128)(2,1)}, bf16[2,384,2560]{1,2,0:T(8,128)(2,1)}, u32[]{:S(2)}, u32[]{:S(2)}) collective-permute-start(bf16[2,384,2560]{1,2,0:T(8,128)(2,1)} %get-tuple-element.175), channel_id=1, source_target_pairs={{8,0},{16,8},{24,16},{32,24},{40,32},{48,40},{56,48},{64,56},{72,6... | collective-permute-start | bytes 11796488 | tf_op jit(solution)/shard_map/ppermute | solution.py:36
  565.9 89.4 %collective-permute-start.3 = (bf16[2,384,2560]{1,2,0:T(8,128)(2,1)}, bf16[2,384,2560]{1,2,0:T(8,128)(2,1)}, u32[]{:S(2)}, u32[]{:S(2)}) collective-permute-start(bf16[2,384,2560]{1,2,0:T(8,128)(2,1)} %get-tuple-element.176), channel_id=1, source_target_pairs={{0,8},{8,16},{16,24},{24,32},{32,40},{40,48},{48,56},{56,64},{64,7... | collective-permute-start | bytes 11796488 | tf_op jit(solution)/shard_map/ppermute | solution.py:36
  582.6 72.8 %slice-start = ((s8[11796480]{0:T(1024)(128)(4,1)}), s8[4194304]{0:T(1024)(128)(4,1)S(1)}, s32[]{:S(2)}) async-start(s8[11796480]{0:T(1024)(128)(4,1)} %bitcast.162), calls=%async_computation.1 | async-start | bytes 8388608
  582.6 72.8 %slice-start.1 = ((s8[11796480]{0:T(1024)(128)(4,1)}), s8[4194304]{0:T(1024)(128)(4,1)S(1)}, s32[]{:S(2)}) async-start(s8[11796480]{0:T(1024)(128)(4,1)} %bitcast.162), calls=%async_computation.2 | async-start | bytes 8388608
  582.6 72.8 %slice-start.2 = ((s8[11796480]{0:T(1024)(128)(4,1)}), s8[3407872]{0:T(1024)(128)(4,1)S(1)}, s32[]{:S(2)}) async-start(s8[11796480]{0:T(1024)(128)(4,1)} %bitcast.162), calls=%async_computation.3 | async-start | bytes 6815744
  665.5 236.7 %copy-start.6 = (bf16[20,384,128]{1,2,0:T(8,128)(2,1)S(1)}, bf16[20,384,128]{1,2,0:T(8,128)(2,1)}, u32[]{:S(2)}) copy-start(bf16[20,384,128]{1,2,0:T(8,128)(2,1)} %get-tuple-element.68) | copy-start | bytes 5898244
  665.5 247.0 %collective-permute-start.4 = (bf16[384,2560]{0,1:T(8,128)(2,1)}, bf16[384,2560]{0,1:T(8,128)(2,1)}, u32[]{:S(2)}, u32[]{:S(2)}) collective-permute-start(bf16[384,2560]{0,1:T(8,128)(2,1)} %fusion.36), channel_id=1, source_target_pairs={{1,0},{2,1},{3,2},{4,3},{5,4},{6,5},{7,6},{9,8},{10,9},{11,10},{12... | collective-permute-start | bytes 5898248 | tf_op jit(solution)/shard_map/ppermute | solution.py:36
  904.6 11.9 %copy-start.1 = (s32[48,7]{0,1:T(8,128)S(1)}, s32[48,7]{0,1:T(8,128)}, u32[]{:S(2)}) copy-start(s32[48,7]{0,1:T(8,128)} %param.14) | copy-start | bytes 4036
  (13 other events, 42.8 us)
Sparse Core Ops, SparseCore 0:
  34.2 140.4 all-reduce.3
where the time goes:
time: 929 us; the launch traced here: 923 us
  matrix products  237 us (26%)
  blocking collectives  235 us (25%)
  waiting for transfers between devices  181 us (19%)
  local copies, waits for them, and re-layouts  158 us (17%)
  other arithmetic  78.9 us (8%)
  starting transfers between devices  17.5 us (2%)
  between operations  14.9 us (2%)
    psum x1, blocking collectives, local(): text_total = lax.psum(dtext_part, 'seq')  235 us
    ppermute x1, waiting for transfers between devices, extended(): lax.ppermute(head, axis, [((i + 1) % count, i) for i in range(ends)])  93.5 us
    dynamic_slice x120, local copies, waits for them, and re-layouts, local(): lax.map(each_head_value, (divide_heads(normed_query), divide_heads(near[0...  68.1 us
    ppermute x3, waiting for transfers between devices, shifted(): return lax.ppermute(x, axis, pairs)  58.7 us
    dot_general x20, matrix products, query_side(): dvals = jnp.dot(probs_b.T, doh, preferred_element_type=jnp.float32)  51.2 us
    dot_general x20, matrix products, query_side(): out = jnp.dot(probs_b, vals, preferred_element_type=jnp.float32)  46 us
    dot_general x20, matrix products, query_side(): dkeys = jnp.dot(dscore.T, qh, preferred_element_type=jnp.float32)  44.5 us
    dot_general x20, matrix products, query_side(): dprob = jnp.dot(doh, vals.T, preferred_element_type=jnp.float32)  38.1 us
  transfers between devices with their start and end apart: 6, of which 5 were waited for; matrix products, arithmetic and copies ran while one was open for 7% of the time, Pallas kernels for 0%

commit v1 on v0

--- a/solution.py
+++ b/solution.py
@@ -1,3 +1,4 @@
+import functools
 import jax
 import jax.numpy as jnp
 from jax import lax
@@ -6,6 +7,25 @@
 HDIM = 128
 BLK = 128
 eps = 1e-06
+
+
+def rounds_advance(content, mesh_dim):
+    n_chips = lax.axis_size(mesh_dim)
+
+    def _lift_task(carry_in, out_arr):
+        if out_arr >= n_chips:
+            return carry_in
+        e_next = lax.ppermute(
+            carry_in,
+            axis_name=mesh_dim,
+            perm=[(dev_j, dev_j ^ out_arr) for dev_j in range(n_chips)],
+        )
+        return _lift_task(carry_in + e_next, 2 * out_arr)
+
+    return _lift_task(content, 1)
+
+
+target_put = functools.partial(rounds_advance, mesh_dim="seq")
 
 
 def extended(cells, sides, width):
@@ -142,7 +162,7 @@
         jnp.float32
     )
     own_rows = ext[:, token_rows : 2 * token_rows] + from_upper + from_lower
-    text_total = lax.psum(dtext_part, "seq")
+    text_total = target_put(dtext_part)
     grad_hidden = (
         own_rows[1]
         + norm_backward(

time: 929 us -> 1650 us (1.78); the launches traced: 923 us -> 1620 us
  waiting for transfers between devices: 181 us -> 1060 us
  blocking collectives: 235 us -> 0 us
  other arithmetic: 78.9 us -> 126 us
    ppermute x0 -> x4, waiting for transfers between devices: none -> 659 us  [_lift_task(): lax.ppermute(carry_in, axis_name=mesh_dim, perm=[(dev_j, dev_j ^ out_arr)...]
    psum x1 -> x0, blocking collectives: 235 us -> none  [local(): text_total = lax.psum(dtext_part, 'seq')]
    ppermute x3, waiting for transfers between devices: 58.7 us -> 279 us  [shifted(): return lax.ppermute(x, axis, pairs)]
    add x0 -> x3, other arithmetic: none -> 39.4 us  [_lift_task(): return _lift_task(carry_in + e_next, 2 * out_arr)]
  transfers between devices with their start and end apart: 6 -> 10, of which waited for: 5 -> 8; matrix products, arithmetic and copies ran while one was open for 7% -> 5% of each run, Pallas kernels for 0% -> 0%
where the time goes in v1:
time: 1650 us; the launch traced here: 1620 us
  waiting for transfers between devices  1060 us (64%)
  matrix products  237 us (14%)
  local copies, waits for them, and re-layouts  158 us (10%)
  other arithmetic  126 us (8%)
  starting transfers between devices  21.7 us (1%)
    ppermute x4, waiting for transfers between devices, _lift_task(): lax.ppermute(carry_in, axis_name=mesh_dim, perm=[(dev_j, dev_j ^ out_arr)...  659 us
    ppermute x3, waiting for transfers between devices, shifted(): return lax.ppermute(x, axis, pairs)  279 us
    ppermute x1, waiting for transfers between devices, extended(): lax.ppermute(head, axis, [((i + 1) % count, i) for i in range(ends)])  93.4 us
    dynamic_slice x120, local copies, waits for them, and re-layouts, local(): lax.map(each_head_value, (divide_heads(normed_query), divide_heads(near[0...  67.8 us
    dot_general x20, matrix products, query_side(): dvals = jnp.dot(probs_b.T, doh, preferred_element_type=jnp.float32)  51.2 us
    dot_general x20, matrix products, query_side(): out = jnp.dot(probs_b, vals, preferred_element_type=jnp.float32)  46 us
    dot_general x20, matrix products, query_side(): dkeys = jnp.dot(dscore.T, qh, preferred_element_type=jnp.float32)  44.5 us
    add x3, other arithmetic, _lift_task(): return _lift_task(carry_in + e_next, 2 * out_arr)  39.4 us
  transfers between devices with their start and end apart: 10, of which 8 were waited for; matrix products, arithmetic and copies ran while one was open for 5% of the time, Pallas kernels for 0%

profile of v1, /device:TPU:24, one launch (start us, length us, event | category | flops | bytes accessed | tf_op | source)
XLA Modules:
  0.0 1619.7 jit_solution(10605565059718131349)
XLA Ops:
  17.4 5.3 collective-permute-start
  23.3 8.0 copy.45
  42.0 93.4 %collective-permute-done.1 = bf16[2,384,2560]{1,2,0:T(8,128)(2,1)} collective-permute-done((bf16[2,384,2560]{1,2,0:T(8,128)(2,1)}, bf16[2,384,2560]{1,2,0:T(8,128)(2,1)}, u32[]{:S(2)}, u32[]{:S(2)}) %collective-permute-start.1) | collective-permute-done | bytes 3932192 | tf_op jit(solution)/shard_map/ppermute | solution.py:41
  138.5 5.1 pad_maximum_fusion.7
  143.6 4.9 fusion.47
  148.5 26.0 %all-reduce.3.cloned.1.call-done = bf16[2,512,2560]{1,2,0:T(8,128)(2,1)} async-done(((bf16[2,512,2560]{1,2,0:T(8,128)(2,1)}), bf16[2,512,2560]{1,2,0:T(8,128)(2,1)}) %all-reduce.3.cloned.1.call-update) | async-done | bytes 5242896 | tf_op jit(solution)/shard_map/psum | solution.py:50
  174.6 5.2 fusion.48
  179.8 351.1 %while.17 = (s32[]{:T(128)}, bf16[20,384,128]{1,2,0:T(8,128)(2,1)}, f32[20,384,128]{1,2,0:T(8,128)}, f32[20,1664,128]{1,2,0:T(8,128)}, f32[20,1664,128]{1,2,0:T(...) while((s32[]{:T(128)}, bf16[20,384,128]{1,2,0:T(8,128)(2,1)}, ...), condition=%wide.region_7.8_spmd.clone, body=%wide.region_3.7_spmd.clone.sunk | while | flops 996523264 | bytes 28792892 | solution.py:145
  534.2 5.2 slice.52
  539.5 5.5 pad_maximum_fusion.8
  545.8 226.6 %collective-permute-done.5 = f32[2,512,2560]{1,2,0:T(8,128)} collective-permute-done((f32[2,512,2560]{1,2,0:T(8,128)}, f32[2,512,2560]{1,2,0:T(8,128)}, u32[]{:S(2)}, u32[]{:S(2)}) %collective-permute-start.5) | collective-permute-done | bytes 10485792 | tf_op jit(solution)/shard_map/ppermute | solution.py:18
  772.5 13.6 fusion.44
  787.5 226.6 %collective-permute-done.6 = f32[2,512,2560]{1,2,0:T(8,128)S(1)} collective-permute-done((f32[2,512,2560]{1,2,0:T(8,128)}, f32[2,512,2560]{1,2,0:T(8,128)S(1)}, u32[]{:S(2)}, u32[]{:S(2)}) %collective-permute-start.6) | collective-permute-done | bytes 10485792 | tf_op jit(solution)/shard_map/ppermute | solution.py:18
  1014.1 12.4 fusion.51
  1026.7 9.7 slice.46
  1036.4 9.8 slice.45
  1046.3 205.8 %collective-permute-done.7 = f32[2,512,2560]{1,2,0:T(8,128)} collective-permute-done((f32[2,512,2560]{1,2,0:T(8,128)}, f32[2,512,2560]{1,2,0:T(8,128)}, u32[]{:S(2)}, u32[]{:S(2)}) %collective-permute-start.7) | collective-permute-done | bytes 10485792 | tf_op jit(solution)/shard_map/ppermute | solution.py:18
  1252.1 13.4 add.71
  1267.0 14.7 fusion.29
  1281.7 6.6 fusion.46
  1291.6 5.2 collective-permute-start.3
  1297.5 278.6 %collective-permute-done.2 = bf16[2,384,2560]{1,2,0:T(8,128)(2,1)} collective-permute-done((bf16[2,384,2560]{1,2,0:T(8,128)(2,1)}, bf16[2,384,2560]{1,2,0:T(8,128)(2,1)}, u32[]{:S(2)}, u32[]{:S(2)}) %collective-permute-start.2) | collective-permute-done | bytes 3932192 | tf_op jit(solution)/shard_map/ppermute | solution.py:56
  1593.8 11.2 fusion.33
  1604.9 7.9 copy.62
  (466 shorter events, 402.9 us)
Async XLA Ops:
  7.2 26.8 %copy-start = (s32[48,7]{0,1:T(8,128)S(1)}, s32[48,7]{0,1:T(8,128)}, u32[]{:S(2)}) copy-start(s32[48,7]{0,1:T(8,128)} %param.14) | copy-start | bytes 4036
  7.2 167.4 %all-reduce.3.cloned.1.call-start = ((), (), s32[]{:S(2)}) async-start(), calls=%async_computation | async-start | bytes 10485760 | tf_op jit(solution)/shard_map/psum | solution.py:50
  14.7 120.7 %collective-permute-start.1 = (bf16[2,384,2560]{1,2,0:T(8,128)(2,1)}, bf16[2,384,2560]{1,2,0:T(8,128)(2,1)}, u32[]{:S(2)}, u32[]{:S(2)}) collective-permute-start(bf16[2,384,2560]{1,2,0:T(8,128)(2,1)} %pad_maximum_fusion.9), channel_id=1, source_target_pairs={{8,0},{16,8},{24,16},{32,24},{40,32},{48,40},{56,48},{64,56},{72,6... | collective-permute-start | bytes 11796488 | tf_op jit(solution)/shard_map/ppermute | solution.py:41
  17.4 121.1 %collective-permute-start = (bf16[2,384,2560]{1,2,0:T(8,128)(2,1)}, bf16[2,384,2560]{1,2,0:T(8,128)(2,1)}, u32[]{:S(2)}, u32[]{:S(2)}) collective-permute-start(bf16[2,384,2560]{1,2,0:T(8,128)(2,1)} %pad_maximum_fusion.9), channel_id=1, source_target_pairs={{0,8},{8,16},{16,24},{24,32},{32,40},{40,48},{48,56},{56,64},{64,7... | collective-permute-start | bytes 11796488 | tf_op jit(solution)/shard_map/ppermute | solution.py:39
  38.7 99.7 %copy-start.5 = (bf16[1,384,2560]{1,2,0:T(8,128)(2,1)S(1)}, bf16[1,384,2560]{1,2,0:T(8,128)(2,1)}, u32[]{:S(2)}) copy-start(bf16[1,384,2560]{1,2,0:T(8,128)(2,1)} %copy-done.4) | copy-start | bytes 5898244
  534.2 5.3 copy-start.2
  539.5 5.5 copy-start.3
  545.0 227.5 %collective-permute-start.5 = (f32[2,512,2560]{1,2,0:T(8,128)}, f32[2,512,2560]{1,2,0:T(8,128)}, u32[]{:S(2)}, u32[]{:S(2)}) collective-permute-start(f32[2,512,2560]{1,2,0:T(8,128)} %pad_maximum_fusion.8), channel_id=1, source_target_pairs={{0,8},{8,0},{16,24},{24,16},{32,40},{40,32},{48,56},{56,48},{64,72... | collective-permute-start | bytes 31457288 | tf_op jit(solution)/shard_map/ppermute | solution.py:18
  786.1 228.0 %collective-permute-start.6 = (f32[2,512,2560]{1,2,0:T(8,128)}, f32[2,512,2560]{1,2,0:T(8,128)S(1)}, u32[]{:S(2)}, u32[]{:S(2)}) collective-permute-start(f32[2,512,2560]{1,2,0:T(8,128)} %fusion.44), channel_id=1, source_target_pairs={{0,16},{8,24},{16,0},{24,8},{32,48},{40,56},{48,32},{56,40},{64,80... | collective-permute-start | bytes 31457288 | tf_op jit(solution)/shard_map/ppermute | solution.py:18
  1026.4 225.7 %collective-permute-start.7 = (f32[2,512,2560]{1,2,0:T(8,128)}, f32[2,512,2560]{1,2,0:T(8,128)}, u32[]{:S(2)}, u32[]{:S(2)}) collective-permute-start(f32[2,512,2560]{1,2,0:T(8,128)} %fusion.51), channel_id=1, source_target_pairs={{0,32},{8,40},{16,48},{24,56},{32,0},{40,8},{48,16},{56,24},{64,96... | collective-permute-start | bytes 31457288 | tf_op jit(solution)/shard_map/ppermute | solution.py:18
  1265.5 328.3 %collective-permute-start.8 = (f32[2,512,2560]{1,2,0:T(8,128)}, f32[2,512,2560]{1,2,0:T(8,128)}, u32[]{:S(2)}, u32[]{:S(2)}) collective-permute-start(f32[2,512,2560]{1,2,0:T(8,128)} %add.71), channel_id=1, source_target_pairs={{0,64},{8,72},{16,80},{24,88},{32,96},{40,104},{48,112},{56,120},{... | collective-permute-start | bytes 31457288 | tf_op jit(solution)/shard_map/ppermute | solution.py:18
  1267.0 29.8 %copy-start.8 = (f32[384,20,128]{0,2,1:T(8,128)S(1)}, f32[384,20,128]{0,2,1:T(8,128)}, u32[]{:S(2)}) copy-start(f32[384,20,128]{0,2,1:T(8,128)} %get-tuple-element.166) | copy-start | bytes 11796484
  1267.0 309.1 %slice-start.3 = ((s8[11796480]{0:T(1024)(128)(4,1)}), s8[4194304]{0:T(1024)(128)(4,1)S(1)}, s32[]{:S(2)}) async-start(s8[11796480]{0:T(1024)(128)(4,1)} %bitcast.165), calls=%async_computation.4 | async-start | bytes 8388608
  1267.0 309.1 %slice-start.4 = ((s8[11796480]{0:T(1024)(128)(4,1)}), s8[4194304]{0:T(1024)(128)(4,1)S(1)}, s32[]{:S(2)}) async-start(s8[11796480]{0:T(1024)(128)(4,1)} %bitcast.165), calls=%async_computation.5 | async-start | bytes 8388608
  1281.7 15.1 copy-start.6
  1281.7 294.4 %slice-start = ((s8[11796480]{0:T(1024)(128)(4,1)}), s8[4194304]{0:T(1024)(128)(4,1)S(1)}, s32[]{:S(2)}) async-start(s8[11796480]{0:T(1024)(128)(4,1)} %bitcast.161), calls=%async_computation.1 | async-start | bytes 8388608
  1281.7 294.4 %slice-start.1 = ((s8[11796480]{0:T(1024)(128)(4,1)}), s8[4194304]{0:T(1024)(128)(4,1)S(1)}, s32[]{:S(2)}) async-start(s8[11796480]{0:T(1024)(128)(4,1)} %bitcast.161), calls=%async_computation.2 | async-start | bytes 8388608
  1281.7 294.4 %slice-start.5 = ((s8[11796480]{0:T(1024)(128)(4,1)}), s8[3407872]{0:T(1024)(128)(4,1)S(1)}, s32[]{:S(2)}) async-start(s8[11796480]{0:T(1024)(128)(4,1)} %bitcast.165), calls=%async_computation.6 | async-start | bytes 6815744
  1288.3 287.7 %collective-permute-start.2 = (bf16[2,384,2560]{1,2,0:T(8,128)(2,1)}, bf16[2,384,2560]{1,2,0:T(8,128)(2,1)}, u32[]{:S(2)}, u32[]{:S(2)}) collective-permute-start(bf16[2,384,2560]{1,2,0:T(8,128)(2,1)} %get-tuple-element.175), channel_id=1, source_target_pairs={{8,0},{16,8},{24,16},{32,24},{40,32},{48,40},{56,48},{64,56},{72,6... | collective-permute-start | bytes 11796488 | tf_op jit(solution)/shard_map/ppermute | solution.py:56
  1291.6 284.5 %collective-permute-start.3 = (bf16[2,384,2560]{1,2,0:T(8,128)(2,1)}, bf16[2,384,2560]{1,2,0:T(8,128)(2,1)}, u32[]{:S(2)}, u32[]{:S(2)}) collective-permute-start(bf16[2,384,2560]{1,2,0:T(8,128)(2,1)} %get-tuple-element.176), channel_id=1, source_target_pairs={{0,8},{8,16},{16,24},{24,32},{32,40},{40,48},{48,56},{56,64},{64,7... | collective-permute-start | bytes 11796488 | tf_op jit(solution)/shard_map/ppermute | solution.py:56
  1296.8 279.3 %slice-start.2 = ((s8[11796480]{0:T(1024)(128)(4,1)}), s8[3407872]{0:T(1024)(128)(4,1)S(1)}, s32[]{:S(2)}) async-start(s8[11796480]{0:T(1024)(128)(4,1)} %bitcast.161), calls=%async_computation.3 | async-start | bytes 6815744
  1297.4 282.7 %copy-start.11 = (f32[2560]{0:T(1024)S(1)}, f32[2560]{0:T(1024)}, u32[]{:S(2)}) copy-start(f32[2560]{0:T(1024)} %copy-done.10) | copy-start | bytes 30724
  1585.3 6.1 collective-permute-start.4
  1593.8 19.1 %copy-start.1 = (s32[48,7]{0,1:T(8,128)S(1)}, s32[48,7]{0,1:T(8,128)}, u32[]{:S(2)}) copy-start(s32[48,7]{0,1:T(8,128)} %param.14) | copy-start | bytes 4036
  (25 other events, 89.9 us)
Sparse Core Ops, SparseCore 0:
  34.1 140.4 all-reduce.2
